TPU v7x, 32 devices: a whole 2x2x4 slice. The times are simulated.
32 devices in a mesh: grp: 2 (over y), ep: 8 (over z, x), sub: 2 (over core).
Axes of the slice: x: 2, y: 2, z: 4, core: 2. Of those that a mesh axis runs over, the one named last changes fastest.
Arguments:
- tokens: bfloat16 [2, 16, 3584], P(None, ('grp', 'ep'), 'sub'), parts along dimension 1, may hold values from -6 to 6
- route_experts: int32 [2, 16, 8], P(None, 'grp'), parts along dimension 1, may hold values from 0 to 15, all different within a row; in each aligned block of 8 rows (0 to 7, 8 to 15, ..., all dimensions but the last counted through in order) at most 6 rows name the same one
- route_weight: float32 [2, 16, 8], P(None, 'grp'), parts along dimension 1, may hold values from 0.05 to 0.6
- expert_slot: int32 [16], replicated, may hold values from 0 to 15, each once
- w_gate: bfloat16 [3584, 32768], P(None, ('ep', 'sub')), may hold values from -0.09375 to 0.09375
- w_up: bfloat16 [3584, 32768], P(None, ('ep', 'sub')), may hold values from -0.09375 to 0.09375
- w_down: bfloat16 [32768, 3584], P(('ep', 'sub')), may hold values from -0.125 to 0.125
Outputs:
- mixed: bfloat16 [2, 16, 3584], P(None, ('grp', 'ep'), 'sub'), parts along dimension 1
There are 2 independent parts, one for each index of `grp`. A program takes and returns all parts, laid end to end along the dimension named above; an argument that names none is the same for every part. Nothing has to cross between parts.
Inputs may be any that keep to these rules, and one draw needn't show every extreme that they name: `route_experts`: in each step no expert is chosen by more than 6 of the 8 tokens, a bound that some block reaches; a token's 8 experts differ. `expert_slot`: each slot holds exactly one expert.
All inputs are finite; a program needn't handle non-finite values.
Results may differ from a plain program's by a relative error of at most 0.005.
Values may be sent and summed in bfloat16 or wider, within the bound.
A program may use at most 128 MiB of HBM per device.

v0:
```python
import jax
import jax.numpy as jnp
from jax import lax
from jax.sharding import PartitionSpec as P

FF = 2048


def swiglu(rows, gate_cols, up_cols, down_rows):
    gate = jnp.dot(rows, gate_cols, preferred_element_type=jnp.float32)
    up = jnp.dot(rows, up_cols, preferred_element_type=jnp.float32)
    hidden = (jax.nn.silu(gate) * up).astype(jnp.bfloat16)
    return jnp.dot(hidden, down_rows, preferred_element_type=jnp.float32)


def expert_terms(rows, experts, weights, expert_slot, w_gate, w_up, w_down, first_col):
    labels = jnp.arange(expert_slot.shape[0], dtype=jnp.int32)
    slot = (first_col + 0) // FF
    logical = jnp.sum(jnp.where(expert_slot == slot, labels, 0))
    chosen = experts == logical
    scale = jnp.sum(jnp.where(chosen, weights, 0.0), axis=1)
    total = scale[:, None] * swiglu(rows, w_gate, w_up, w_down)
    return total


def collect(local):
    gathered = lax.all_gather(local, "ep", axis=0, tiled=True)
    return lax.all_gather(gathered, "sub", axis=1, tiled=True)


def spread(total):
    owned = lax.psum_scatter(total, "ep", scatter_dimension=0, tiled=True)
    return lax.psum_scatter(owned, "sub", scatter_dimension=1, tiled=True)


def on_device(tokens, route_experts, route_weight, expert_slot, w_gate, w_up, w_down):
    sub_size = lax.axis_size("sub")
    first_col = (lax.axis_index("ep") * sub_size + lax.axis_index("sub")) * w_gate.shape[1]
    results = []
    for step in range(tokens.shape[0]):
        rows = collect(tokens[step])
        total = expert_terms(
            rows,
            route_experts[step],
            route_weight[step],
            expert_slot,
            w_gate,
            w_up,
            w_down,
            first_col,
        )
        results.append(spread(total).astype(jnp.bfloat16))
    return jnp.stack(results)


def solution(mesh):
    return jax.shard_map(
        on_device,
        mesh=mesh,
        in_specs=(
            P(None, ("grp", "ep"), "sub"),
            P(None, "grp", None),
            P(None, "grp", None),
            P(),
            P(None, ("ep", "sub")),
            P(None, ("ep", "sub")),
            P(("ep", "sub"), None),
        ),
        out_specs=P(None, ("grp", "ep"), "sub"),
        check_vma=False,
    )
```

profile of v0, /device:TPU:1, one launch (start us, length us, event | category | flops | bytes accessed | tf_op | source)
XLA Modules:
  0.0 214.1 jit_solution(6319772681553025402)
XLA Ops:
  6.5 0.0 all-reduce.5.cloned.1.call-start
  6.5 0.9 slice_bitcast_fusion.1
  7.4 25.7 %all-gather = bf16[8,1,1792]{2,1,0:T(2,128)(2,1)S(1)} all-gather(bf16[1,1,1792]{2,1,0:T(2,128)(2,1)S(1)} %get-tuple-element.9), channel_id=2, replica_groups=mesh['grp'=2,'ep'=8,'sub'=2] {'ep'}, dimensions={0}, use_global_device_ids=true | all-gather | bytes 32256 | tf_op jit(solution)/shard_map/all_gather | solution.py:27
  33.2 8.4 %all-gather.1 = bf16[8,1,3584]{2,0,1:T(8,128)(2,1)S(1)} all-gather(bf16[8,1,1792]{2,0,1:T(8,128)(2,1)S(1)} %copy.11), channel_id=3, replica_groups=mesh['grp'=2,'ep'=8,'sub'=2] {'sub'}, dimensions={2}, use_global_device_ids=true | all-gather | bytes 86016 | tf_op jit(solution)/shard_map/all_gather | solution.py:28
  41.5 24.2 %all-gather.2 = bf16[8,1,1792]{2,1,0:T(2,128)(2,1)S(1)} all-gather(bf16[1,1,1792]{2,1,0:T(2,128)(2,1)S(1)} %get-tuple-element.10), channel_id=4, replica_groups=mesh['grp'=2,'ep'=8,'sub'=2] {'ep'}, dimensions={0}, use_global_device_ids=true | all-gather | bytes 32256 | tf_op jit(solution)/shard_map/all_gather | solution.py:27
  65.8 8.2 %all-gather.3 = bf16[8,1,3584]{2,0,1:T(8,128)(2,1)S(1)} all-gather(bf16[8,1,1792]{2,0,1:T(8,128)(2,1)S(1)} %copy.13), channel_id=5, replica_groups=mesh['grp'=2,'ep'=8,'sub'=2] {'sub'}, dimensions={2}, use_global_device_ids=true | all-gather | bytes 86016 | tf_op jit(solution)/shard_map/all_gather | solution.py:28
  74.0 7.2 %fusion.14 = f32[8,2048]{1,0:T(8,128)S(1)} fusion(bf16[3584,2048]{1,0:T(8,128)(2,1)} %param.11, bf16[8,1,3584]{2,0,1:T(8,128)(2,1)S(1)} %all-gather.3), kind=kOutput, calls=%fused_computation.19 | convolution fusion | flops 117440512 | bytes 14802944 | tf_op jit(solution)/shard_map/dot_general | solution.py:10
  81.2 0.0 copy-done
  81.2 0.0 copy-start.2
  81.2 2.0 fusion.18
  83.2 0.6 fusion.22
  83.8 0.0 copy-done.1
  83.8 0.8 select_reduce_fusion.1
  84.6 12.0 %convolution_multiply_fusion = f32[8,3584]{1,0:T(8,128)} fusion(bf16[2048,3584]{1,0:T(8,128)(2,1)} %param.13, bf16[3584,2048]{1,0:T(8,128)(2,1)} %param.12, f32[8,2048]{1,0:T(8,128)S(1)} %fusion.14, bf16[8,1,3584]{2,0,1:T(8,128)(2,1)S(1)} %all-gather.3, f32[8]{0:T(128)S(1)} %get-tuple-element.6), kind=kOutput, calls=%fused_computation | convolution fusion | flops 235008000 | bytes 29597728 | tf_op jit(solution)/shard_map/dot_general | solution.py:13
  96.7 12.0 %convolution_multiply_fusion.1 = f32[8,3584]{1,0:T(8,128)} fusion(bf16[2048,3584]{1,0:T(8,128)(2,1)} %param.13, bf16[3584,2048]{1,0:T(8,128)(2,1)} %param.12, f32[8,2048]{1,0:T(8,128)S(1)} %fusion.18, bf16[8,1,3584]{2,0,1:T(8,128)(2,1)S(1)} %all-gather.1, f32[8]{0:T(128)S(1)} %get-tuple-element.5), kind=kOutput, calls=%fused_computation.1 | convolution fusion | flops 235008000 | bytes 29597728 | tf_op jit(solution)/shard_map/dot_general | solution.py:13
  108.7 0.0 all-reduce.5.cloned.1.call-update
  108.7 0.0 reduce-scatter.9.cloned.1.call-start
  108.8 0.6 dynamic-slice
  109.4 68.9 %all-reduce.5.cloned.1.call-done = (f32[8,3584]{1,0:T(8,128)}, f32[8,3584]{1,0:T(8,128)}) async-done(((f32[8,3584]{1,0:T(8,128)}, f32[8,3584]{1,0:T(8,128)}), (f32[8,3584]{1,0:T(8,128)}, f32[8,3584]{1,0:T(8,128)})) %all-reduce.5.cloned.1.call-update) | async-done | bytes 229392
  178.3 1.6 constant_dynamic-slice_fusion
  179.9 1.8 copy.16
  181.8 0.0 reduce-scatter.9.cloned.1.call-update
  181.8 0.0 reduce-scatter.7.cloned.1.call-start
  181.8 1.8 copy.14
  183.6 0.0 reduce-scatter.7.cloned.1.call-update
  183.7 9.1 %reduce-scatter.9.cloned.1.call-done = f32[1792,1]{1,0:T(8,128)} async-done(((f32[3584,1]{1,0:T(8,128)}), f32[1792,1]{1,0:T(8,128)}) %reduce-scatter.9.cloned.1.call-update) | async-done | bytes 7184
  192.7 1.2 convert_bitcast_fusion
  194.0 0.2 copy.21
  194.2 11.4 %reduce-scatter.7.cloned.1.call-done = f32[1792,1]{1,0:T(8,128)} async-done(((f32[3584,1]{1,0:T(8,128)}), f32[1792,1]{1,0:T(8,128)}) %reduce-scatter.7.cloned.1.call-update) | async-done | bytes 7184
  205.5 1.2 convert_bitcast_fusion.1
  206.8 0.2 copy.20
  207.0 0.6 pad_maximum_fusion
  (9 shorter events, 0.0 us)
Async XLA Ops:
  6.5 171.7 %all-reduce.5.cloned.1.call-start = ((), (), s32[]{:S(2)}) async-start(), calls=%async_computation.4 | async-start | bytes 458752
  6.5 74.6 %copy-start = (bf16[3584,2048]{1,0:T(8,128)(2,1)S(1)}, bf16[3584,2048]{1,0:T(8,128)(2,1)}, u32[]{:S(2)}) copy-start(bf16[3584,2048]{1,0:T(8,128)(2,1)} %param.11) | copy-start | bytes 44040196
  81.2 2.0 copy-start.3
  81.2 2.7 %copy-start.1 = (f32[2,8,8]{2,1,0:T(8,128)S(1)}, f32[2,8,8]{2,1,0:T(8,128)}, u32[]{:S(2)}) copy-start(f32[2,8,8]{2,1,0:T(8,128)} %param.9) | copy-start | bytes 1540
  81.2 2.7 %copy-start.2 = (s32[2,8,8]{2,1,0:T(8,128)S(1)}, s32[2,8,8]{2,1,0:T(8,128)}, u32[]{:S(2)}) copy-start(s32[2,8,8]{2,1,0:T(8,128)} %param.8) | copy-start | bytes 1540
  96.7 12.1 %copy-start.4 = (u32[32]{0:T(128)S(1)}, u32[32]{0:T(128)}, u32[]{:S(2)}) copy-start(u32[32]{0:T(128)} %constant.39) | copy-start | bytes 388
  108.7 84.0 %reduce-scatter.9.cloned.1.call-start = ((), (), s32[]{:S(2)}) async-start(), calls=%async_computation.3 | async-start | bytes 2752512
  181.8 23.8 %reduce-scatter.7.cloned.1.call-start = ((), (), s32[]{:S(2)}) async-start(), calls=%async_computation.2 | async-start | bytes 2752512
Sparse Core Ops, SparseCore 0:
  108.8 69.3 all-reduce.4
  181.9 10.7 reduce-scatter.8
  195.0 10.5 reduce-scatter.6
where the time goes:
time: 215 us; the launch traced here: 214 us
  waiting for transfers between devices  89.4 us (42%)
  blocking collectives  66.6 us (31%)
  matrix products  33.2 us (15%)
  between operations  13.2 us (6%)
  local copies, waits for them, and re-layouts  7.19 us (3%)
  other arithmetic  4.5 us (2%)
    unnamed x6, waiting for transfers between devices  89.4 us
    all_gather x2, blocking collectives, collect(): gathered = lax.all_gather(local, 'ep', axis=0, tiled=True)  50 us
    dot_general x2, matrix products, swiglu(): return jnp.dot(hidden, down_rows, preferred_element_type=jnp.float32)  24.1 us
    all_gather x2, blocking collectives, collect(): return lax.all_gather(gathered, 'sub', axis=1, tiled=True)  16.6 us
    dot_general x2, matrix products, swiglu(): gate = jnp.dot(rows, gate_cols, preferred_element_type=jnp.float32)  9.17 us
    unnamed x17, local copies, waits for them, and re-layouts  7.18 us
  transfers between devices with their start and end apart: 3, of which 3 were waited for; matrix products, arithmetic and copies ran while one was open for 2% of the time, Pallas kernels for 0%

commit v1 on v0

--- a/solution.py
+++ b/solution.py
@@ -1,9 +1,14 @@
 import jax
 import jax.numpy as jnp
 from jax import lax
+from jax.experimental import pallas as pl
+from jax.experimental.pallas import tpu as pltpu
 from jax.sharding import PartitionSpec as P
 
 FF = 2048
+LANES = 128
+BLOCK = 256
+MESH = pl.DeviceIdType.MESH
 
 
 def swiglu(rows, gate_cols, up_cols, down_rows):
@@ -33,14 +38,15 @@
     return lax.psum_scatter(owned, "sub", scatter_dimension=1, tiled=True)
 
 
-def on_device(tokens, route_experts, route_weight, expert_slot, w_gate, w_up, w_down):
+def with_collectives(tokens, route_experts, route_weight, expert_slot, w_gate, w_up, w_down):
     sub_size = lax.axis_size("sub")
     first_col = (lax.axis_index("ep") * sub_size + lax.axis_index("sub")) * w_gate.shape[1]
+    steps, count, part = tokens.shape
+    rows = jnp.stack([collect(tokens[step]) for step in range(steps)])
     results = []
-    for step in range(tokens.shape[0]):
-        rows = collect(tokens[step])
+    for step in range(steps):
         total = expert_terms(
-            rows,
+            rows[step],
             route_experts[step],
             route_weight[step],
             expert_slot,
@@ -51,6 +57,298 @@
         )
         results.append(spread(total).astype(jnp.bfloat16))
     return jnp.stack(results)
+
+
+def layer_kernel(
+    peers,
+    sub_size,
+    slots_ref,
+    tokens_ref,
+    experts_ref,
+    weights_ref,
+    gate_ref,
+    up_ref,
+    down_ref,
+    out_ref,
+    tok,
+    exp_in,
+    wt_in,
+    stage,
+    mine,
+    gathered,
+    wide,
+    rows,
+    gates,
+    ups,
+    downs,
+    hidden,
+    spreadout,
+    sendbuf,
+    landed,
+    small_sem,
+    gate_sem,
+    up_sem,
+    down_sem,
+    tok_send,
+    tok_recv,
+    sum_send,
+    sum_recv,
+):
+    steps, _, part = tokens_ref.shape
+    ep_size = peers // sub_size
+    pad = stage.shape[0] // steps
+    cols = part // LANES
+    n_up = gates.shape[0]
+    n_half = part // BLOCK
+    grp = lax.axis_index("grp")
+    my_ep = lax.axis_index("ep")
+    my_sub = lax.axis_index("sub")
+    me = my_ep * sub_size + my_sub
+
+    barrier = pltpu.get_barrier_semaphore()
+
+    def greet(o, carry):
+        peer = lax.rem(me + o, peers)
+        pl.semaphore_signal(
+            barrier,
+            inc=1,
+            device_id=(grp, peer // sub_size, lax.rem(peer, sub_size)),
+            device_id_type=MESH,
+        )
+        return carry
+
+    lax.fori_loop(1, peers, greet, 0)
+
+    small = [
+        pltpu.make_async_copy(tokens_ref, tok, small_sem.at[0]),
+        pltpu.make_async_copy(experts_ref, exp_in, small_sem.at[1]),
+        pltpu.make_async_copy(weights_ref, wt_in, small_sem.at[2]),
+    ]
+    for copy in small:
+        copy.start()
+
+    def gate_copy(c):
+        at = pl.multiple_of(c * BLOCK, BLOCK)
+        return pltpu.make_async_copy(gate_ref.at[:, pl.ds(at, BLOCK)], gates.at[c], gate_sem.at[c])
+
+    def up_copy(c):
+        at = pl.multiple_of(c * BLOCK, BLOCK)
+        return pltpu.make_async_copy(up_ref.at[:, pl.ds(at, BLOCK)], ups.at[c], up_sem.at[c])
+
+    def down_copy(c):
+        at = pl.multiple_of(c * BLOCK, BLOCK)
+        return pltpu.make_async_copy(down_ref.at[:, pl.ds(at, BLOCK)], downs.at[c], down_sem.at[c])
+
+    def start_up(c, carry):
+        gate_copy(c).start()
+        up_copy(c).start()
+        return carry
+
+    def start_down(c, carry):
+        down_copy(c).start()
+        return carry
+
+    lax.fori_loop(0, n_up, start_up, 0)
+    lax.fori_loop(0, downs.shape[0], start_down, 0)
+
+    for copy in small:
+        copy.wait()
+    stage[...] = jnp.zeros_like(stage)
+    for t in range(steps):
+        row = tok[t].astype(jnp.float32)
+        for c in range(cols):
+            stage[t * pad + c : t * pad + c + 1, :] = row[:, c * LANES : (c + 1) * LANES]
+    mine[...] = stage[...].astype(jnp.bfloat16)
+    gathered[me] = mine[...]
+
+    pl.semaphore_wait(barrier, peers - 1)
+
+    def token_copy(peer, slot):
+        return pltpu.make_async_remote_copy(
+            src_ref=mine,
+            dst_ref=gathered.at[slot],
+            send_sem=tok_send.at[peer],
+            recv_sem=tok_recv.at[slot],
+            device_id=(grp, peer // sub_size, lax.rem(peer, sub_size)),
+            device_id_type=MESH,
+        )
+
+    def send_tokens(o, carry):
+        token_copy(lax.rem(me + o, peers), me).start()
+        return carry
+
+    lax.fori_loop(1, peers, send_tokens, 0)
+
+    logical = jnp.int32(0)
+    for e in range(slots_ref.shape[0]):
+        logical += jnp.where(slots_ref[e] == me, jnp.int32(e), jnp.int32(0))
+    scales = [
+        jnp.sum(
+            jnp.where(exp_in[t] == logical, wt_in[t], 0.0), axis=1, keepdims=True
+        )
+        for t in range(steps)
+    ]
+
+    def land_tokens(o, carry):
+        peer = lax.rem(me + o, peers)
+        token_copy(peer, peer).wait_recv()
+        return carry
+
+    lax.fori_loop(1, peers, land_tokens, 0)
+    wide[...] = gathered[...].astype(jnp.float32).reshape(wide.shape)
+    for s in range(sub_size):
+        for c in range(cols):
+            picked = [
+                wide[pl.ds(s * steps * pad + t * pad + c, ep_size, stride=sub_size * steps * pad), :]
+                for t in range(steps)
+            ]
+            at = s * part + c * LANES
+            rows[:, at : at + LANES] = jnp.concatenate(picked, axis=0).astype(jnp.bfloat16)
+
+    def hide(c, carry):
+        gate_copy(c).wait()
+        up_copy(c).wait()
+        gate = jnp.dot(rows[...], gates[c], preferred_element_type=jnp.float32)
+        up = jnp.dot(rows[...], ups[c], preferred_element_type=jnp.float32)
+        value = gate / (1.0 + jnp.exp(-gate)) * up
+        hidden[:, pl.ds(pl.multiple_of(c * BLOCK, BLOCK), BLOCK)] = value.astype(jnp.bfloat16)
+        return carry
+
+    lax.fori_loop(0, n_up, hide, 0)
+
+    spreadout[...] = jnp.zeros_like(spreadout)
+
+    def sum_copy(owner, slot):
+        return pltpu.make_async_remote_copy(
+            src_ref=sendbuf.at[owner],
+            dst_ref=landed.at[slot],
+            send_sem=sum_send.at[owner],
+            recv_sem=sum_recv.at[slot],
+            device_id=(grp, owner // sub_size, lax.rem(owner, sub_size)),
+            device_id_type=MESH,
+        )
+
+    for s in range(sub_size):
+
+        def lower(n, carry):
+            down_copy(s * n_half + n).wait()
+            value = jnp.dot(hidden[...], downs[s * n_half + n], preferred_element_type=jnp.float32)
+            for t in range(steps):
+                term = value[t * ep_size : (t + 1) * ep_size] * scales[t]
+                for k in range(BLOCK // LANES):
+                    start = t * pad + n * (BLOCK // LANES) + k
+                    spreadout[pl.ds(start, ep_size, stride=steps * pad), :] = term[
+                        :, k * LANES : (k + 1) * LANES
+                    ]
+            return carry
+
+        lax.fori_loop(0, n_half, lower, 0)
+
+        def send_sums(o, carry):
+            j = lax.rem(my_ep + o, ep_size)
+            owner = j * sub_size + s
+            first = pl.multiple_of(j * steps * pad, steps * pad)
+            block = spreadout[pl.ds(first, steps * pad), :].astype(jnp.bfloat16)
+
+            @pl.when(owner == me)
+            def _():
+                landed[me] = block
+
+            @pl.when(owner != me)
+            def _():
+                sendbuf[owner] = block
+                sum_copy(owner, me).start()
+
+            return carry
+
+        lax.fori_loop(1, ep_size + 1, send_sums, 0)
+
+    def land_sums(o, carry):
+        peer = lax.rem(me + o, peers)
+        sum_copy(peer, peer).wait_recv()
+        return carry
+
+    lax.fori_loop(1, peers, land_sums, 0)
+    total = landed[0].astype(jnp.float32)
+    for p in range(1, peers):
+        total += landed[p].astype(jnp.float32)
+    out_ref[...] = total.astype(jnp.bfloat16)
+
+    def sent(o, carry):
+        peer = lax.rem(me + o, peers)
+        token_copy(peer, me).wait_send()
+        sum_copy(peer, me).wait_send()
+        return carry
+
+    lax.fori_loop(1, peers, sent, 0)
+
+
+def with_kernel(tokens, route_experts, route_weight, expert_slot, w_gate, w_up, w_down):
+    sub_size = lax.axis_size("sub")
+    ep_size = lax.axis_size("ep")
+    peers = sub_size * ep_size
+    steps, _, part = tokens.shape
+    depth, width = w_gate.shape
+    cols = part // LANES
+    pad = -(-cols // 16) * 16
+    block = steps * pad
+    bf16, f32 = jnp.bfloat16, jnp.float32
+    dma = pltpu.SemaphoreType.DMA
+
+    def body(*refs):
+        layer_kernel(peers, sub_size, *refs)
+
+    out = pl.pallas_call(
+        body,
+        out_shape=jax.ShapeDtypeStruct((block, LANES), bf16),
+        in_specs=[pl.BlockSpec(memory_space=pltpu.SMEM)] + [pl.BlockSpec(memory_space=pl.ANY)] * 6,
+        out_specs=pl.BlockSpec(memory_space=pltpu.VMEM),
+        scratch_shapes=[
+            pltpu.VMEM(tokens.shape, bf16),
+            pltpu.VMEM(route_experts.shape, jnp.int32),
+            pltpu.VMEM(route_weight.shape, f32),
+            pltpu.VMEM((block, LANES), f32),
+            pltpu.VMEM((block, LANES), bf16),
+            pltpu.VMEM((peers, block, LANES), bf16),
+            pltpu.VMEM((peers * block, LANES), f32),
+            pltpu.VMEM((steps * ep_size, depth), bf16),
+            pltpu.VMEM((width // BLOCK, depth, BLOCK), bf16),
+            pltpu.VMEM((width // BLOCK, depth, BLOCK), bf16),
+            pltpu.VMEM((depth // BLOCK, width, BLOCK), bf16),
+            pltpu.VMEM((steps * ep_size, width), bf16),
+            pltpu.VMEM((ep_size * block, LANES), f32),
+            pltpu.VMEM((peers, block, LANES), bf16),
+            pltpu.VMEM((peers, block, LANES), bf16),
+            dma((3,)),
+            dma((width // BLOCK,)),
+            dma((width // BLOCK,)),
+            dma((depth // BLOCK,)),
+            dma((peers,)),
+            dma((peers,)),
+            dma((peers,)),
+            dma((peers,)),
+        ],
+        compiler_params=pltpu.CompilerParams(
+            collective_id=0, has_side_effects=True, vmem_limit_bytes=56 * 1024 * 1024
+        ),
+        cost_estimate=pl.CostEstimate(
+            flops=6 * steps * ep_size * depth * width,
+            bytes_accessed=6 * depth * width,
+            transcendentals=steps * ep_size * width,
+        ),
+    )(expert_slot, tokens, route_experts, route_weight, w_gate, w_up, w_down)
+    return out.reshape(steps, pad, LANES)[:, :cols].reshape(steps, 1, part)
+
+
+def on_device(tokens, route_experts, route_weight, expert_slot, w_gate, w_up, w_down):
+    fits = (
+        w_gate.shape[1] == FF
+        and tokens.shape[1] == 1
+        and tokens.shape[2] % BLOCK == 0
+        and lax.axis_size("ep") == 8
+    )
+    plan = with_kernel if fits else with_collectives
+    return plan(tokens, route_experts, route_weight, expert_slot, w_gate, w_up, w_down)
 
 
 def solution(mesh):

time: 215 us -> 29 us (0.13)
  waiting for transfers between devices: 89.4 us -> 0 us
  blocking collectives: 66.6 us -> 0 us
  matrix products: 33.2 us -> 0 us
  Pallas kernels: 0 us -> 26.1 us
  between operations: 13.2 us -> 0.01 us
  local copies, waits for them, and re-layouts: 7.19 us -> 2.61 us
  other arithmetic: 4.5 us -> 0 us
    unnamed x6 -> x0, waiting for transfers between devices: 89.4 us -> none
    all_gather x4 -> x0, blocking collectives: 66.6 us -> none  [the longest x2 50 us: collect(): gathered = lax.all_gather(local, 'ep', axis=0, tiled=True)]
    dot_general x4 -> x0, matrix products: 33.2 us -> none  [the longest x2 24.1 us: swiglu(): return jnp.dot(hidden, down_rows, preferred_element_type=jnp.float32)]
    pallas_call x0 -> x1, Pallas kernels: none -> 26.1 us  [with_kernel(): pl.pallas_call(body, out_shape=jax.ShapeDtypeStruct((block, LANES), bf16)...]
    unnamed x17 -> x1, local copies, waits for them, and re-layouts: 7.18 us -> 1.3 us
    unnamed x2 -> x0, other arithmetic: 2.45 us -> none
  transfers between devices with their start and end apart: 3 -> 0, of which waited for: 3 -> 0; matrix products, arithmetic and copies ran while one was open for 2% -> 0% of each run, Pallas kernels for 0% -> 0%
where the time goes in v1:
time: 29 us; the launch traced here: 28.7 us
  Pallas kernels  26.1 us (90%)
  local copies, waits for them, and re-layouts  2.61 us (9%)
    pallas_call x1, Pallas kernels, with_kernel(): pl.pallas_call(body, out_shape=jax.ShapeDtypeStruct((block, LANES), bf16)...  26.1 us
    reshape x1, local copies, waits for them, and re-layouts, with_kernel(): return out.reshape(steps, pad, LANES)[:, :cols].reshape(steps, 1, part)  1.31 us
    unnamed x1, local copies, waits for them, and re-layouts  1.3 us

profile of v1, /device:TPU:1, one launch (start us, length us, event | category | flops | bytes accessed | tf_op | source)
XLA Modules:
  0.0 28.7 jit_solution(3167670871980843584)
XLA Ops:
  0.0 1.3 %copy.9.refs_1_ = bf16[2,1,1792]{2,1,0:T(2,128)(2,1)} copy(bf16[2,1,1792]{2,0,1:T(2,128)(2,1)} %param.7) | data formatting | bytes 14336 | tf_op args[0]
  1.3 26.1 %shard_map.73 = bf16[32,128]{1,0:T(8,128)(2,1)} custom-call(s32[16]{0:T(128)} %refs_0_.1, bf16[2,1,1792]{2,1,0:T(2,128)(2,1)} %copy.9.refs_1_, s32[2,8,8]{2,1,0:T(8,128)} %refs_2_.1, f32[2,8,8]{2,1,0:T(8,128)} %refs_3_.1, bf16[3584,2048]{1,0:T(8,128)(2,1)} %refs_4_.1, bf16[3584,2048]{1,0:T(8,128)(2,1)} %refs_5_.1, bf16[2048,3584]{1,0:T(8,128)(2,1)} %refs_6_.1), custom_call_target="tpu_custom_call" | custom-call | flops 704643072 | bytes 44040192 | tf_op jit(solution)/shard_map/pallas_call | solution.py:301
  27.4 1.3 %reshape.7 = bf16[2,1,1792]{2,0,1:T(2,128)(2,1)} reshape(bf16[2,14,128]{2,1,0:T(8,128)(2,1)} %bitcast.2) | data formatting | bytes 14336 | tf_op jit(solution)/shard_map/reshape | solution.py:340

commit v2 on v1

--- a/solution.py
+++ b/solution.py
@@ -7,7 +7,8 @@
 
 FF = 2048
 LANES = 128
-BLOCK = 256
+UP_BLOCK = 512
+DOWN_BLOCK = 1792
 MESH = pl.DeviceIdType.MESH
 
 
@@ -70,6 +71,7 @@
     up_ref,
     down_ref,
     out_ref,
+    slots,
     tok,
     exp_in,
     wt_in,
@@ -94,12 +96,12 @@
     sum_send,
     sum_recv,
 ):
-    steps, _, part = tokens_ref.shape
+    steps, part = tokens_ref.shape
     ep_size = peers // sub_size
     pad = stage.shape[0] // steps
     cols = part // LANES
     n_up = gates.shape[0]
-    n_half = part // BLOCK
+    n_half = part // DOWN_BLOCK
     grp = lax.axis_index("grp")
     my_ep = lax.axis_index("ep")
     my_sub = lax.axis_index("sub")
@@ -123,21 +125,22 @@
         pltpu.make_async_copy(tokens_ref, tok, small_sem.at[0]),
         pltpu.make_async_copy(experts_ref, exp_in, small_sem.at[1]),
         pltpu.make_async_copy(weights_ref, wt_in, small_sem.at[2]),
+        pltpu.make_async_copy(slots_ref, slots, small_sem.at[3]),
     ]
     for copy in small:
         copy.start()
 
     def gate_copy(c):
-        at = pl.multiple_of(c * BLOCK, BLOCK)
-        return pltpu.make_async_copy(gate_ref.at[:, pl.ds(at, BLOCK)], gates.at[c], gate_sem.at[c])
+        at = pl.multiple_of(c * UP_BLOCK, UP_BLOCK)
+        return pltpu.make_async_copy(gate_ref.at[:, pl.ds(at, UP_BLOCK)], gates.at[c], gate_sem.at[c])
 
     def up_copy(c):
-        at = pl.multiple_of(c * BLOCK, BLOCK)
-        return pltpu.make_async_copy(up_ref.at[:, pl.ds(at, BLOCK)], ups.at[c], up_sem.at[c])
+        at = pl.multiple_of(c * UP_BLOCK, UP_BLOCK)
+        return pltpu.make_async_copy(up_ref.at[:, pl.ds(at, UP_BLOCK)], ups.at[c], up_sem.at[c])
 
     def down_copy(c):
-        at = pl.multiple_of(c * BLOCK, BLOCK)
-        return pltpu.make_async_copy(down_ref.at[:, pl.ds(at, BLOCK)], downs.at[c], down_sem.at[c])
+        at = pl.multiple_of(c * DOWN_BLOCK, DOWN_BLOCK)
+        return pltpu.make_async_copy(down_ref.at[:, pl.ds(at, DOWN_BLOCK)], downs.at[c], down_sem.at[c])
 
     def start_up(c, carry):
         gate_copy(c).start()
@@ -151,11 +154,10 @@
     lax.fori_loop(0, n_up, start_up, 0)
     lax.fori_loop(0, downs.shape[0], start_down, 0)
 
-    for copy in small:
-        copy.wait()
     stage[...] = jnp.zeros_like(stage)
+    small[0].wait()
     for t in range(steps):
-        row = tok[t].astype(jnp.float32)
+        row = tok[t : t + 1, :].astype(jnp.float32)
         for c in range(cols):
             stage[t * pad + c : t * pad + c + 1, :] = row[:, c * LANES : (c + 1) * LANES]
     mine[...] = stage[...].astype(jnp.bfloat16)
@@ -179,9 +181,13 @@
 
     lax.fori_loop(1, peers, send_tokens, 0)
 
+    spreadout[...] = jnp.zeros_like(spreadout)
+    for copy in small[1:]:
+        copy.wait()
+
     logical = jnp.int32(0)
-    for e in range(slots_ref.shape[0]):
-        logical += jnp.where(slots_ref[e] == me, jnp.int32(e), jnp.int32(0))
+    for e in range(slots.shape[0]):
+        logical += jnp.where(slots[e] == me, jnp.int32(e), jnp.int32(0))
     scales = [
         jnp.sum(
             jnp.where(exp_in[t] == logical, wt_in[t], 0.0), axis=1, keepdims=True
@@ -211,12 +217,10 @@
         gate = jnp.dot(rows[...], gates[c], preferred_element_type=jnp.float32)
         up = jnp.dot(rows[...], ups[c], preferred_element_type=jnp.float32)
         value = gate / (1.0 + jnp.exp(-gate)) * up
-        hidden[:, pl.ds(pl.multiple_of(c * BLOCK, BLOCK), BLOCK)] = value.astype(jnp.bfloat16)
+        hidden[:, pl.ds(pl.multiple_of(c * UP_BLOCK, UP_BLOCK), UP_BLOCK)] = value.astype(jnp.bfloat16)
         return carry
 
     lax.fori_loop(0, n_up, hide, 0)
-
-    spreadout[...] = jnp.zeros_like(spreadout)
 
     def sum_copy(owner, slot):
         return pltpu.make_async_remote_copy(
@@ -235,8 +239,8 @@
             value = jnp.dot(hidden[...], downs[s * n_half + n], preferred_element_type=jnp.float32)
             for t in range(steps):
                 term = value[t * ep_size : (t + 1) * ep_size] * scales[t]
-                for k in range(BLOCK // LANES):
-                    start = t * pad + n * (BLOCK // LANES) + k
+                for k in range(DOWN_BLOCK // LANES):
+                    start = t * pad + n * (DOWN_BLOCK // LANES) + k
                     spreadout[pl.ds(start, ep_size, stride=steps * pad), :] = term[
                         :, k * LANES : (k + 1) * LANES
                     ]
@@ -272,7 +276,10 @@
     total = landed[0].astype(jnp.float32)
     for p in range(1, peers):
         total += landed[p].astype(jnp.float32)
-    out_ref[...] = total.astype(jnp.bfloat16)
+    for t in range(steps):
+        at = t * pad
+        row = jnp.concatenate([total[at + c : at + c + 1] for c in range(cols)], axis=1)
+        out_ref[t : t + 1, :] = row.astype(jnp.bfloat16)
 
     def sent(o, carry):
         peer = lax.rem(me + o, peers)
@@ -300,11 +307,12 @@
 
     out = pl.pallas_call(
         body,
-        out_shape=jax.ShapeDtypeStruct((block, LANES), bf16),
-        in_specs=[pl.BlockSpec(memory_space=pltpu.SMEM)] + [pl.BlockSpec(memory_space=pl.ANY)] * 6,
+        out_shape=jax.ShapeDtypeStruct((steps, part), bf16),
+        in_specs=[pl.BlockSpec(memory_space=pl.ANY)] * 7,
         out_specs=pl.BlockSpec(memory_space=pltpu.VMEM),
         scratch_shapes=[
-            pltpu.VMEM(tokens.shape, bf16),
+            pltpu.SMEM(expert_slot.shape, jnp.int32),
+            pltpu.VMEM((steps, part), bf16),
             pltpu.VMEM(route_experts.shape, jnp.int32),
             pltpu.VMEM(route_weight.shape, f32),
             pltpu.VMEM((block, LANES), f32),
@@ -312,17 +320,17 @@
             pltpu.VMEM((peers, block, LANES), bf16),
             pltpu.VMEM((peers * block, LANES), f32),
             pltpu.VMEM((steps * ep_size, depth), bf16),
-            pltpu.VMEM((width // BLOCK, depth, BLOCK), bf16),
-            pltpu.VMEM((width // BLOCK, depth, BLOCK), bf16),
-            pltpu.VMEM((depth // BLOCK, width, BLOCK), bf16),
+            pltpu.VMEM((width // UP_BLOCK, depth, UP_BLOCK), bf16),
+            pltpu.VMEM((width // UP_BLOCK, depth, UP_BLOCK), bf16),
+            pltpu.VMEM((depth // DOWN_BLOCK, width, DOWN_BLOCK), bf16),
             pltpu.VMEM((steps * ep_size, width), bf16),
             pltpu.VMEM((ep_size * block, LANES), f32),
             pltpu.VMEM((peers, block, LANES), bf16),
             pltpu.VMEM((peers, block, LANES), bf16),
-            dma((3,)),
-            dma((width // BLOCK,)),
-            dma((width // BLOCK,)),
-            dma((depth // BLOCK,)),
+            dma((4,)),
+            dma((width // UP_BLOCK,)),
+            dma((width // UP_BLOCK,)),
+            dma((depth // DOWN_BLOCK,)),
             dma((peers,)),
             dma((peers,)),
             dma((peers,)),
@@ -336,15 +344,15 @@
             bytes_accessed=6 * depth * width,
             transcendentals=steps * ep_size * width,
         ),
-    )(expert_slot, tokens, route_experts, route_weight, w_gate, w_up, w_down)
-    return out.reshape(steps, pad, LANES)[:, :cols].reshape(steps, 1, part)
+    )(expert_slot, tokens.reshape(steps, part), route_experts, route_weight, w_gate, w_up, w_down)
+    return out.reshape(steps, 1, part)
 
 
 def on_device(tokens, route_experts, route_weight, expert_slot, w_gate, w_up, w_down):
     fits = (
         w_gate.shape[1] == FF
         and tokens.shape[1] == 1
-        and tokens.shape[2] % BLOCK == 0
+        and tokens.shape[2] % DOWN_BLOCK == 0
         and lax.axis_size("ep") == 8
     )
     plan = with_kernel if fits else with_collectives

time: 29 us -> 25.2 us (0.87)
  Pallas kernels: 26.1 us -> 23.6 us
  local copies, waits for them, and re-layouts: 2.61 us -> 1.29 us
    pallas_call x1, Pallas kernels: 26.1 us -> 23.6 us  [with_kernel(): pl.pallas_call(body, out_shape=jax.ShapeDtypeStruct((steps, part), bf16),...]
    reshape x1 -> x0, local copies, waits for them, and re-layouts: 1.31 us -> none  [with_kernel(): return out.reshape(steps, pad, LANES)[:, :cols].reshape(steps, 1, part)]
where the time goes in v2:
time: 25.2 us; the launch traced here: 24.9 us
  Pallas kernels  23.6 us (94%)
  local copies, waits for them, and re-layouts  1.29 us (5%)
    pallas_call x1, Pallas kernels, with_kernel(): pl.pallas_call(body, out_shape=jax.ShapeDtypeStruct((steps, part), bf16),...  23.6 us
    unnamed x1, local copies, waits for them, and re-layouts  1.29 us

profile of v2, /device:TPU:1, one launch (start us, length us, event | category | flops | bytes accessed | tf_op | source)
XLA Modules:
  0.0 24.9 jit_solution(2175553108934839545)
XLA Ops:
  0.0 23.6 %shard_map.73 = bf16[2,1792]{1,0:T(2,128)(2,1)} custom-call(s32[16]{0:T(128)} %refs_0_.1, bf16[2,1792]{1,0:T(2,128)(2,1)} %bitcast.3, s32[2,8,8]{2,1,0:T(8,128)} %refs_2_.1, f32[2,8,8]{2,1,0:T(8,128)} %refs_3_.1, bf16[3584,2048]{1,0:T(8,128)(2,1)} %refs_4_.1, bf16[3584,2048]{1,0:T(8,128)(2,1)} %refs_5_.1, bf16[2048,3584]{1,0:T(8,128)(2,1)} %refs_6_.1), custom_call_target="tpu_custom_call" | custom-call | flops 704643072 | bytes 44040192 | tf_op jit(solution)/shard_map/pallas_call | solution.py:308
  23.6 1.3 %copy.9 = bf16[2,1,1792]{2,0,1:T(2,128)(2,1)} copy(bf16[2,1,1792]{2,0,1:T(2,128)(2,1)} %bitcast.2) | data formatting | bytes 14336

commit v3 on v2

--- a/solution.py
+++ b/solution.py
@@ -7,7 +7,7 @@
 
 FF = 2048
 LANES = 128
-UP_BLOCK = 512
+UP_BLOCK = 1024
 DOWN_BLOCK = 1792
 MESH = pl.DeviceIdType.MESH
 
@@ -119,7 +119,7 @@
         )
         return carry
 
-    lax.fori_loop(1, peers, greet, 0)
+    lax.fori_loop(1, peers, greet, 0, unroll=True)
 
     small = [
         pltpu.make_async_copy(tokens_ref, tok, small_sem.at[0]),
@@ -151,7 +151,7 @@
         down_copy(c).start()
         return carry
 
-    lax.fori_loop(0, n_up, start_up, 0)
+    lax.fori_loop(0, n_up, start_up, 0, unroll=True)
     lax.fori_loop(0, downs.shape[0], start_down, 0)
 
     stage[...] = jnp.zeros_like(stage)
@@ -179,7 +179,7 @@
         token_copy(lax.rem(me + o, peers), me).start()
         return carry
 
-    lax.fori_loop(1, peers, send_tokens, 0)
+    lax.fori_loop(1, peers, send_tokens, 0, unroll=True)
 
     spreadout[...] = jnp.zeros_like(spreadout)
     for copy in small[1:]:
@@ -200,7 +200,7 @@
         token_copy(peer, peer).wait_recv()
         return carry
 
-    lax.fori_loop(1, peers, land_tokens, 0)
+    lax.fori_loop(1, peers, land_tokens, 0, unroll=True)
     wide[...] = gathered[...].astype(jnp.float32).reshape(wide.shape)
     for s in range(sub_size):
         for c in range(cols):
@@ -220,7 +220,7 @@
         hidden[:, pl.ds(pl.multiple_of(c * UP_BLOCK, UP_BLOCK), UP_BLOCK)] = value.astype(jnp.bfloat16)
         return carry
 
-    lax.fori_loop(0, n_up, hide, 0)
+    lax.fori_loop(0, n_up, hide, 0, unroll=True)
 
     def sum_copy(owner, slot):
         return pltpu.make_async_remote_copy(
@@ -265,14 +265,14 @@
 
             return carry
 
-        lax.fori_loop(1, ep_size + 1, send_sums, 0)
+        lax.fori_loop(1, ep_size + 1, send_sums, 0, unroll=True)
 
     def land_sums(o, carry):
         peer = lax.rem(me + o, peers)
         sum_copy(peer, peer).wait_recv()
         return carry
 
-    lax.fori_loop(1, peers, land_sums, 0)
+    lax.fori_loop(1, peers, land_sums, 0, unroll=True)
     total = landed[0].astype(jnp.float32)
     for p in range(1, peers):
         total += landed[p].astype(jnp.float32)
@@ -287,7 +287,7 @@
         sum_copy(peer, me).wait_send()
         return carry
 
-    lax.fori_loop(1, peers, sent, 0)
+    lax.fori_loop(1, peers, sent, 0, unroll=True)
 
 
 def with_kernel(tokens, route_experts, route_weight, expert_slot, w_gate, w_up, w_down):

time: 25.2 us -> 24.7 us (0.980)
  Pallas kernels: 23.6 us -> 23.2 us
    pallas_call x1, Pallas kernels: 23.6 us -> 23.2 us  [with_kernel(): pl.pallas_call(body, out_shape=jax.ShapeDtypeStruct((steps, part), bf16),...]
where the time goes in v3:
time: 24.7 us; the launch traced here: 24.5 us
  Pallas kernels  23.2 us (94%)
  local copies, waits for them, and re-layouts  1.29 us (5%)
    pallas_call x1, Pallas kernels, with_kernel(): pl.pallas_call(body, out_shape=jax.ShapeDtypeStruct((steps, part), bf16),...  23.2 us
    unnamed x1, local copies, waits for them, and re-layouts  1.29 us

profile of v3, /device:TPU:1, one launch (start us, length us, event | category | flops | bytes accessed | tf_op | source)
XLA Modules:
  0.0 24.5 jit_solution(14217544321364976707)
XLA Ops:
  0.0 23.2 %shard_map.73 = bf16[2,1792]{1,0:T(2,128)(2,1)} custom-call(s32[16]{0:T(128)} %refs_0_.1, bf16[2,1792]{1,0:T(2,128)(2,1)} %bitcast.3, s32[2,8,8]{2,1,0:T(8,128)} %refs_2_.1, f32[2,8,8]{2,1,0:T(8,128)} %refs_3_.1, bf16[3584,2048]{1,0:T(8,128)(2,1)} %refs_4_.1, bf16[3584,2048]{1,0:T(8,128)(2,1)} %refs_5_.1, bf16[2048,3584]{1,0:T(8,128)(2,1)} %refs_6_.1), custom_call_target="tpu_custom_call" | custom-call | flops 704643072 | bytes 44040192 | tf_op jit(solution)/shard_map/pallas_call | solution.py:308
  23.2 1.3 %copy.9 = bf16[2,1,1792]{2,0,1:T(2,128)(2,1)} copy(bf16[2,1,1792]{2,0,1:T(2,128)(2,1)} %bitcast.2) | data formatting | bytes 14336

commit v4 on v3

--- a/solution.py
+++ b/solution.py
@@ -222,6 +222,12 @@
 
     lax.fori_loop(0, n_up, hide, 0, unroll=True)
 
+    def tokens_sent(o, carry):
+        token_copy(lax.rem(me + o, peers), me).wait_send()
+        return carry
+
+    lax.fori_loop(1, peers, tokens_sent, 0, unroll=True)
+
     def sum_copy(owner, slot):
         return pltpu.make_async_remote_copy(
             src_ref=sendbuf.at[owner],
@@ -279,15 +285,17 @@
     for t in range(steps):
         at = t * pad
         row = jnp.concatenate([total[at + c : at + c + 1] for c in range(cols)], axis=1)
-        out_ref[t : t + 1, :] = row.astype(jnp.bfloat16)
+        tok[t : t + 1, :] = row.astype(jnp.bfloat16)
+    result = pltpu.make_async_copy(tok, out_ref, small_sem.at[0])
+    result.start()
 
     def sent(o, carry):
         peer = lax.rem(me + o, peers)
-        token_copy(peer, me).wait_send()
         sum_copy(peer, me).wait_send()
         return carry
 
     lax.fori_loop(1, peers, sent, 0, unroll=True)
+    result.wait()
 
 
 def with_kernel(tokens, route_experts, route_weight, expert_slot, w_gate, w_up, w_down):
@@ -309,7 +317,7 @@
         body,
         out_shape=jax.ShapeDtypeStruct((steps, part), bf16),
         in_specs=[pl.BlockSpec(memory_space=pl.ANY)] * 7,
-        out_specs=pl.BlockSpec(memory_space=pltpu.VMEM),
+        out_specs=pl.BlockSpec(memory_space=pl.ANY),
         scratch_shapes=[
             pltpu.SMEM(expert_slot.shape, jnp.int32),
             pltpu.VMEM((steps, part), bf16),

time: 24.7 us -> 24.7 us (level)
  no operation moved by 1% of the time
where the time goes in v4:
time: 24.7 us; the launch traced here: 24.5 us
  Pallas kernels  23.1 us (94%)
  local copies, waits for them, and re-layouts  1.29 us (5%)
    pallas_call x1, Pallas kernels, with_kernel(): pl.pallas_call(body, out_shape=jax.ShapeDtypeStruct((steps, part), bf16),...  23.1 us
    unnamed x1, local copies, waits for them, and re-layouts  1.29 us

profile of v4, /device:TPU:1, one launch (start us, length us, event | category | flops | bytes accessed | tf_op | source)
XLA Modules:
  0.0 24.5 jit_solution(8357932502002195265)
XLA Ops:
  0.0 23.1 %shard_map.73 = bf16[2,1792]{1,0:T(2,128)(2,1)} custom-call(s32[16]{0:T(128)} %refs_0_.1, bf16[2,1792]{1,0:T(2,128)(2,1)} %bitcast.3, s32[2,8,8]{2,1,0:T(8,128)} %refs_2_.1, f32[2,8,8]{2,1,0:T(8,128)} %refs_3_.1, bf16[3584,2048]{1,0:T(8,128)(2,1)} %refs_4_.1, bf16[3584,2048]{1,0:T(8,128)(2,1)} %refs_5_.1, bf16[2048,3584]{1,0:T(8,128)(2,1)} %refs_6_.1), custom_call_target="tpu_custom_call" | custom-call | flops 704643072 | bytes 44040192 | tf_op jit(solution)/shard_map/pallas_call | solution.py:316
  23.2 1.3 %copy.9 = bf16[2,1,1792]{2,0,1:T(2,128)(2,1)} copy(bf16[2,1,1792]{2,0,1:T(2,128)(2,1)} %bitcast.2) | data formatting | bytes 14336
